TPU v7x, 32 devices: a whole 2x2x4 slice. The times are simulated.
32 devices in a mesh: dp: 16 (over z, x, core), tensor: 2 (over y).
Axes of the slice: x: 2, y: 2, z: 4, core: 2. Of those that a mesh axis runs over, the one named last changes fastest.
Arguments:
- tokens: bfloat16 [8192, 768], P('dp'), may hold values from -6 to 6
- w_qkv: bfloat16 [2, 768, 3, 768], P(None, None, None, 'tensor'), may hold values from -0.21875 to 0.21875
- w_out: bfloat16 [2, 768, 768], P(None, 'tensor'), may hold values from -0.875 to 0.875
- w_up: bfloat16 [2, 768, 3072], P(None, None, 'tensor'), may hold values from -0.21875 to 0.21875
- w_down: bfloat16 [2, 3072, 768], P(None, 'tensor'), may hold values from -0.109375 to 0.109375
- norm_gain: float32 [2, 2, 768], replicated, may hold values from 0.5 to 1.5
- norm_shift: float32 [2, 2, 768], replicated, may hold values from -1.5 to 1.5
- d_out: bfloat16 [8192, 768], P('dp'), may hold values from -6 to 6
Outputs:
- out_one: bfloat16 [8192, 768], P('dp')
- out_two: bfloat16 [8192, 768], P('dp')
- input_grad: float32 [8192, 768], P('dp')
- grad_qkv: float32 [2, 768, 3, 768], P(None, None, None, 'tensor')
- grad_out: float32 [2, 768, 768], P(None, 'tensor')
- grad_up: float32 [2, 768, 3072], P(None, None, 'tensor')
- grad_down: float32 [2, 3072, 768], P(None, 'tensor')
- grad_gain: float32 [2, 2, 768], replicated
- grad_shift: float32 [2, 2, 768], replicated
All inputs are finite; a program needn't handle non-finite values.
Results may differ from a plain program's by a relative error of at most 0.028.
Values may be sent and summed in bfloat16 or wider, within the bound.
No kernel may reach another device: no remote copies, remote signals or barrier semaphores. Data moves between devices by JAX's collectives and lax.ppermute only.
A program may use at most 192 MiB of HBM per device.

v0:
```python
import jax
import jax.numpy as jnp
from jax import lax
from jax.sharding import PartitionSpec as P

HEAD_DIM = 64


SOFTNESS = 0.25
EPSILON = 1e-05


def norm_rows(rows_in, gain, shift):
    row_mean = jnp.mean(rows_in, axis=-1, keepdims=True)
    centered = rows_in - row_mean
    spread = jnp.mean(centered * centered, axis=-1, keepdims=True)
    return centered * lax.rsqrt(spread + EPSILON) * gain + shift


def smooth_gelu(values_in):
    return jax.nn.gelu(values_in, approximate=True)


def block_scores(query_block, keys_all, block_start, signed):
    block_len, head_count, head_size = query_block.shape
    length = keys_all.shape[0]
    scores = jnp.einsum(
        "qhd,khd->hqk", query_block, keys_all, preferred_element_type=jnp.float32
    ) * head_size ** (-0.5)
    row_ids = block_start + jnp.arange(block_len, dtype=jnp.int32)
    col_ids = jnp.arange(length, dtype=jnp.int32)
    allowed = (col_ids[None, :] <= row_ids[:, None])[None]
    if signed:
        magnitude = jnp.sqrt(scores * scores + SOFTNESS * SOFTNESS)
    else:
        magnitude = scores
    masked = jnp.where(allowed, magnitude, -1e30)
    return (scores, magnitude, masked, allowed)


def split_blocks(queries):
    length, head_count, head_size = queries.shape
    block_len = min(512, length)
    num_blocks = length // block_len
    block_starts = jnp.arange(num_blocks, dtype=jnp.int32) * block_len
    return (queries.reshape(num_blocks, block_len, head_count, head_size), block_starts)


def attend_forward(queries, keys_all, values_in, signed):
    query_blocks, block_starts = split_blocks(queries)

    def one_block(element):
        query_block, block_start = element
        scores, magnitude, masked, allowed = block_scores(
            query_block, keys_all, block_start, signed
        )
        peak = jnp.max(masked, axis=-1, keepdims=True)
        exponent = jnp.where(allowed, jnp.exp(masked - peak), 0.0)
        row_total = jnp.sum(exponent, axis=-1, keepdims=True)
        softmax_part = exponent / row_total
        if signed:
            weights = softmax_part * (scores / magnitude)
        else:
            weights = softmax_part
        attended = jnp.einsum(
            "hqk,khd->qhd",
            weights.astype(jnp.bfloat16),
            values_in,
            preferred_element_type=jnp.float32,
        )
        return (attended.astype(jnp.bfloat16), (peak + jnp.log(row_total))[..., 0])

    attended, log_sums = lax.map(one_block, (query_blocks, block_starts))
    length, head_count, head_size = queries.shape
    return (attended.reshape(length, head_count * head_size), log_sums)


def attend_backward(queries, keys_all, values_in, log_sums, d_att, signed):
    query_blocks, block_starts = split_blocks(queries)
    d_blocks = d_att.reshape(query_blocks.shape)
    head_size = queries.shape[2]
    scale = head_size ** (-0.5)

    def one_block(carried, element):
        d_keys, d_values = carried
        query_block, d_block, block_sum, block_start = element
        scores, magnitude, masked, allowed = block_scores(
            query_block, keys_all, block_start, signed
        )
        softmax_part = jnp.where(allowed, jnp.exp(masked - block_sum[:, :, None]), 0.0)
        if signed:
            sign_part = scores / magnitude
            weights = softmax_part * sign_part
        else:
            weights = softmax_part
        prob_low = weights.astype(jnp.bfloat16)
        d_probs = jnp.einsum("qhd,khd->hqk", d_block, values_in, preferred_element_type=jnp.float32)
        d_values = d_values + jnp.einsum(
            "hqk,qhd->khd", prob_low, d_block, preferred_element_type=jnp.float32
        )
        delta = jnp.sum(weights * d_probs, axis=-1, keepdims=True)
        if signed:
            bend = sign_part * sign_part + SOFTNESS * SOFTNESS / (magnitude * magnitude * magnitude)
            d_scores = softmax_part * d_probs * bend - weights * delta
        else:
            d_scores = softmax_part * (d_probs - delta)
        d_low = d_scores.astype(jnp.bfloat16)
        d_query = (
            jnp.einsum("hqk,khd->qhd", d_low, keys_all, preferred_element_type=jnp.float32) * scale
        )
        d_keys = (
            d_keys
            + jnp.einsum("hqk,qhd->khd", d_low, query_block, preferred_element_type=jnp.float32)
            * scale
        )
        return ((d_keys, d_values), d_query)

    zeros = jnp.zeros(keys_all.shape, jnp.float32)
    (d_keys, d_values), d_queries = lax.scan(
        one_block, (zeros, zeros), (query_blocks, d_blocks, log_sums, block_starts)
    )
    return (
        d_queries.reshape(queries.shape).astype(jnp.bfloat16),
        d_keys.astype(jnp.bfloat16),
        d_values.astype(jnp.bfloat16),
    )


def layer_forward(resid_in, w_qkv, w_out, w_up, w_down, gain, shift, signed):
    length = resid_in.shape[0]
    width_part = w_qkv.shape[2]
    head_shape = (length, width_part // HEAD_DIM, HEAD_DIM)
    normed_one = norm_rows(resid_in, gain[0], shift[0]).astype(jnp.bfloat16)
    projected = jnp.einsum(
        "ld,dcf->lcf", normed_one, w_qkv, preferred_element_type=jnp.float32
    ).astype(jnp.bfloat16)
    queries = projected[:, 0].reshape(head_shape)
    keys_all = projected[:, 1].reshape(head_shape)
    values_in = projected[:, 2].reshape(head_shape)
    attended, log_sums = attend_forward(queries, keys_all, values_in, signed)
    branch_share = lax.psum_scatter(
        jnp.dot(attended, w_out, preferred_element_type=jnp.float32).astype(jnp.bfloat16),
        "tensor",
        scatter_dimension=0,
        tiled=True,
    ).astype(jnp.float32)
    branch = lax.all_gather(branch_share.astype(jnp.bfloat16), "tensor", axis=0, tiled=True).astype(
        branch_share.dtype
    )
    middle = resid_in + branch
    normed_two = norm_rows(middle, gain[1], shift[1]).astype(jnp.bfloat16)
    pre_act = jnp.dot(normed_two, w_up, preferred_element_type=jnp.float32)
    hidden = smooth_gelu(pre_act).astype(jnp.bfloat16)
    mixed_share = lax.psum_scatter(
        jnp.dot(hidden, w_down, preferred_element_type=jnp.float32).astype(jnp.bfloat16),
        "tensor",
        scatter_dimension=0,
        tiled=True,
    ).astype(jnp.float32)
    mixed = lax.all_gather(mixed_share.astype(jnp.bfloat16), "tensor", axis=0, tiled=True).astype(
        mixed_share.dtype
    )
    saved = (
        resid_in,
        normed_one,
        queries,
        keys_all,
        values_in,
        attended,
        log_sums,
        middle,
        normed_two,
        pre_act,
        hidden,
    )
    return (middle + mixed, saved)


def layer_backward(d_next, saved, w_qkv, w_out, w_up, w_down, gain, shift, signed):
    (
        resid_in,
        normed_one,
        queries,
        keys_all,
        values_in,
        attended,
        log_sums,
        middle,
        normed_two,
        pre_act,
        hidden,
    ) = saved
    length = resid_in.shape[0]
    d_low = d_next.astype(jnp.bfloat16)
    g_down = jnp.einsum("lf,ld->fd", hidden, d_low, preferred_element_type=jnp.float32)
    d_hidden = jnp.einsum("ld,fd->lf", d_low, w_down, preferred_element_type=jnp.float32)
    gelu_out, gelu_pull = jax.vjp(smooth_gelu, pre_act)
    d_pre = gelu_pull(d_hidden)[0].astype(jnp.bfloat16)
    g_up = jnp.einsum("ld,lf->df", normed_two, d_pre, preferred_element_type=jnp.float32)
    two_share = lax.psum_scatter(
        jnp.einsum("lf,df->ld", d_pre, w_up, preferred_element_type=jnp.float32).astype(
            jnp.bfloat16
        ),
        "tensor",
        scatter_dimension=0,
        tiled=True,
    ).astype(jnp.float32)
    d_normed_two = lax.all_gather(
        two_share.astype(jnp.bfloat16), "tensor", axis=0, tiled=True
    ).astype(two_share.dtype)
    norm_out, norm_pull = jax.vjp(norm_rows, middle, gain[1], shift[1])
    d_mid_part, g_gain_two, g_shift_two = norm_pull(d_normed_two)
    d_middle = d_next + d_mid_part
    d_mid_low = d_middle.astype(jnp.bfloat16)
    g_out = jnp.einsum("lf,ld->fd", attended, d_mid_low, preferred_element_type=jnp.float32)
    d_att = jnp.einsum("ld,fd->lf", d_mid_low, w_out, preferred_element_type=jnp.float32).astype(
        jnp.bfloat16
    )
    d_query, d_key, d_value = attend_backward(queries, keys_all, values_in, log_sums, d_att, signed)
    width_part = w_qkv.shape[2]
    d_qkv = jnp.stack(
        [
            d_query.reshape(length, width_part),
            d_key.reshape(length, width_part),
            d_value.reshape(length, width_part),
        ],
        axis=1,
    )
    g_qkv = jnp.einsum("ld,lcf->dcf", normed_one, d_qkv, preferred_element_type=jnp.float32)
    one_share = lax.psum_scatter(
        jnp.einsum("lcf,dcf->ld", d_qkv, w_qkv, preferred_element_type=jnp.float32).astype(
            jnp.bfloat16
        ),
        "tensor",
        scatter_dimension=0,
        tiled=True,
    ).astype(jnp.float32)
    d_normed_one = lax.all_gather(
        one_share.astype(jnp.bfloat16), "tensor", axis=0, tiled=True
    ).astype(one_share.dtype)
    first_out, first_pull = jax.vjp(norm_rows, resid_in, gain[0], shift[0])
    d_in_part, g_gain_one, g_shift_one = first_pull(d_normed_one)
    grad_parts = (
        g_qkv,
        g_out,
        g_up,
        g_down,
        jnp.stack([g_gain_one, g_gain_two]),
        jnp.stack([g_shift_one, g_shift_two]),
    )
    return (d_middle + d_in_part, grad_parts)


def on_device(tokens, w_qkv, w_out, w_up, w_down, norm_gain, norm_shift, d_out):
    layer_count = w_qkv.shape[0]
    stream = tokens.astype(jnp.float32)
    saved_list = []
    outputs = []
    for layer_idx in range(layer_count):
        stream, saved = layer_forward(
            stream,
            w_qkv[layer_idx],
            w_out[layer_idx],
            w_up[layer_idx],
            w_down[layer_idx],
            norm_gain[layer_idx],
            norm_shift[layer_idx],
            layer_idx == 0,
        )
        saved_list.append(saved)
        outputs.append(stream)
    gradient = d_out.astype(jnp.float32)
    layer_grads = [None] * layer_count
    for layer_idx in reversed(range(layer_count)):
        gradient, grad_parts = layer_backward(
            gradient,
            saved_list[layer_idx],
            w_qkv[layer_idx],
            w_out[layer_idx],
            w_up[layer_idx],
            w_down[layer_idx],
            norm_gain[layer_idx],
            norm_shift[layer_idx],
            layer_idx == 0,
        )
        layer_grads[layer_idx] = grad_parts
    stacked = tuple((jnp.stack([parts[member] for parts in layer_grads]) for member in range(6)))
    shares = (
        lax.psum_scatter(stacked[0], "dp", scatter_dimension=1, tiled=True),
        lax.psum_scatter(stacked[1], "dp", scatter_dimension=2, tiled=True),
        lax.psum_scatter(stacked[2], "dp", scatter_dimension=1, tiled=True),
        lax.psum_scatter(stacked[3], "dp", scatter_dimension=2, tiled=True),
        lax.psum_scatter(stacked[4], "dp", scatter_dimension=2, tiled=True),
        lax.psum_scatter(stacked[5], "dp", scatter_dimension=2, tiled=True),
    )
    stacked = (
        lax.all_gather(shares[0].astype(jnp.bfloat16), "dp", axis=1, tiled=True).astype(
            jnp.float32
        ),
        lax.all_gather(shares[1].astype(jnp.bfloat16), "dp", axis=2, tiled=True).astype(
            jnp.float32
        ),
        lax.all_gather(shares[2].astype(jnp.bfloat16), "dp", axis=1, tiled=True).astype(
            jnp.float32
        ),
        lax.all_gather(shares[3].astype(jnp.bfloat16), "dp", axis=2, tiled=True).astype(
            jnp.float32
        ),
        lax.all_gather(shares[4].astype(jnp.bfloat16), "dp", axis=2, tiled=True).astype(
            jnp.float32
        ),
        lax.all_gather(shares[5].astype(jnp.bfloat16), "dp", axis=2, tiled=True).astype(
            jnp.float32
        ),
    )
    return (
        outputs[0].astype(jnp.bfloat16),
        outputs[1].astype(jnp.bfloat16),
        gradient,
        stacked[0],
        stacked[1],
        stacked[2],
        stacked[3],
        stacked[4],
        stacked[5],
    )


def solution(mesh):
    in_specs = (
        P("dp", None),
        P(None, None, None, "tensor"),
        P(None, "tensor", None),
        P(None, None, "tensor"),
        P(None, "tensor", None),
        P(),
        P(),
        P("dp", None),
    )
    out_specs = (
        P("dp", None),
        P("dp", None),
        P("dp", None),
        P(None, None, None, "tensor"),
        P(None, "tensor", None),
        P(None, None, "tensor"),
        P(None, "tensor", None),
        P(),
        P(),
    )
    return jax.shard_map(
        on_device, mesh=mesh, in_specs=in_specs, out_specs=out_specs, check_vma=False
    )
```

profile of v0, /device:TPU:9, one launch (start us, length us, event | category | flops | bytes accessed | tf_op | source)
XLA Modules:
  0.0 1033.0 jit_solution(4531965168745885613)
XLA Ops:
  28.4 18.7 %reduce-scatter.17.cloned.1.call-done = bf16[256,768]{1,0:T(8,128)(2,1)} async-done(((bf16[512,768]{1,0:T(8,128)(2,1)}), bf16[256,768]{1,0:T(8,128)(2,1)}) %reduce-scatter.17.cloned.1.call-update) | async-done | bytes 393232 | tf_op jit(solution)/shard_map/reduce_scatter | solution.py:141
  47.1 10.9 %all_gather.42 = bf16[512,768]{1,0:T(8,128)(2,1)S(1)} all-gather(bf16[256,768]{1,0:T(8,128)(2,1)} %reduce-scatter.17.cloned.1.call-done), channel_id=1, replica_groups=mesh['dp'=16,'tensor'=2] {'tensor'}, dimensions={0}, use_global_device_ids=true | all-gather | bytes 1179648 | tf_op jit(solution)/shard_map/all_gather | solution.py:147
  66.6 18.4 %reduce-scatter.19.cloned.1.call-done = bf16[256,768]{1,0:T(8,128)(2,1)} async-done(((bf16[512,768]{1,0:T(8,128)(2,1)}), bf16[256,768]{1,0:T(8,128)(2,1)}) %reduce-scatter.19.cloned.1.call-update) | async-done | bytes 393232 | tf_op jit(solution)/shard_map/reduce_scatter | solution.py:154
  85.0 11.0 %all_gather.43 = bf16[512,768]{1,0:T(8,128)(2,1)S(1)} all-gather(bf16[256,768]{1,0:T(8,128)(2,1)} %reduce-scatter.19.cloned.1.call-done), channel_id=1, replica_groups=mesh['dp'=16,'tensor'=2] {'tensor'}, dimensions={0}, use_global_device_ids=true | all-gather | bytes 1179648 | tf_op jit(solution)/shard_map/all_gather | solution.py:160
  107.8 18.4 %reduce-scatter.21.cloned.1.call-done = bf16[256,768]{1,0:T(8,128)(2,1)} async-done(((bf16[512,768]{1,0:T(8,128)(2,1)}), bf16[256,768]{1,0:T(8,128)(2,1)}) %reduce-scatter.21.cloned.1.call-update) | async-done | bytes 393232 | tf_op jit(solution)/shard_map/reduce_scatter | solution.py:141
  126.2 10.8 %all_gather.44 = bf16[512,768]{1,0:T(8,128)(2,1)S(1)} all-gather(bf16[256,768]{1,0:T(8,128)(2,1)} %reduce-scatter.21.cloned.1.call-done), channel_id=1, replica_groups=mesh['dp'=16,'tensor'=2] {'tensor'}, dimensions={0}, use_global_device_ids=true | all-gather | bytes 1179648 | tf_op jit(solution)/shard_map/all_gather | solution.py:147
  149.0 5.4 fusion.111
  154.5 12.7 %reduce-scatter.25.cloned.1.call-done = bf16[256,768]{1,0:T(8,128)(2,1)} async-done(((bf16[512,768]{1,0:T(8,128)(2,1)}), bf16[256,768]{1,0:T(8,128)(2,1)}) %reduce-scatter.25.cloned.1.call-update) | async-done | bytes 393232 | tf_op jit(solution)/shard_map/reduce_scatter | solution.py:200
  167.2 10.9 %all_gather.46 = bf16[512,768]{1,0:T(8,128)(2,1)S(1)} all-gather(bf16[256,768]{1,0:T(8,128)(2,1)} %reduce-scatter.25.cloned.1.call-done), channel_id=1, replica_groups=mesh['dp'=16,'tensor'=2] {'tensor'}, dimensions={0}, use_global_device_ids=true | all-gather | bytes 1179648 | tf_op jit(solution)/shard_map/all_gather | solution.py:208
  181.0 7.6 reduce-scatter.23.cloned.1.call-done
  188.6 11.3 %all_gather.45 = bf16[512,768]{1,0:T(8,128)(2,1)S(1)} all-gather(bf16[256,768]{1,0:T(8,128)(2,1)} %reduce-scatter.23.cloned.1.call-done), channel_id=1, replica_groups=mesh['dp'=16,'tensor'=2] {'tensor'}, dimensions={0}, use_global_device_ids=true | all-gather | bytes 1179648 | tf_op jit(solution)/shard_map/all_gather | solution.py:160
  226.2 18.1 %reduce-scatter.27.cloned.1.call-done = bf16[256,768]{1,0:T(8,128)(2,1)} async-done(((bf16[512,768]{1,0:T(8,128)(2,1)}), bf16[256,768]{1,0:T(8,128)(2,1)}) %reduce-scatter.27.cloned.1.call-update) | async-done | bytes 393232 | tf_op jit(solution)/shard_map/reduce_scatter | solution.py:230
  244.4 11.2 %all_gather.47 = bf16[512,768]{1,0:T(8,128)(2,1)S(1)} all-gather(bf16[256,768]{1,0:T(8,128)(2,1)} %reduce-scatter.27.cloned.1.call-done), channel_id=1, replica_groups=mesh['dp'=16,'tensor'=2] {'tensor'}, dimensions={0}, use_global_device_ids=true | all-gather | bytes 1179648 | tf_op jit(solution)/shard_map/all_gather | solution.py:238
  267.7 18.4 %reduce-scatter.29.cloned.1.call-done = bf16[256,768]{1,0:T(8,128)(2,1)} async-done(((bf16[512,768]{1,0:T(8,128)(2,1)}), bf16[256,768]{1,0:T(8,128)(2,1)}) %reduce-scatter.29.cloned.1.call-update) | async-done | bytes 393232 | tf_op jit(solution)/shard_map/reduce_scatter | solution.py:200
  286.2 11.0 %all_gather.48 = bf16[512,768]{1,0:T(8,128)(2,1)S(1)} all-gather(bf16[256,768]{1,0:T(8,128)(2,1)} %reduce-scatter.29.cloned.1.call-done), channel_id=1, replica_groups=mesh['dp'=16,'tensor'=2] {'tensor'}, dimensions={0}, use_global_device_ids=true | all-gather | bytes 1179648 | tf_op jit(solution)/shard_map/all_gather | solution.py:208
  301.5 5.6 fusion.121
  307.1 5.7 multiply_reduce_fusion
  312.9 6.6 fusion.6
  364.8 15.5 %copy.58 = f32[2,1536,768]{1,0,2:T(2,128)} copy(f32[2,1536,768]{2,1,0:T(8,128)} %pad_maximum_fusion.1) | data formatting | bytes 18874368 | tf_op jit(solution)/shard_map/stack | solution.py:287
  388.6 298.8 %all-reduce.4 = (bf16[2,384,768]{1,0,2:T(2,128)(2,1)}, bf16[2,1536,768]{1,0,2:T(2,128)(2,1)}) all-reduce(f32[2,384,768]{1,0,2:T(2,128)} %copy.57, f32[2,1536,768]{1,0,2:T(2,128)} %copy.58), channel_id=11, replica_groups=mesh['dp'=16,'tensor'=2] {'dp'}, use_global_device_ids=true, to_apply=%region_31.32.clone | all-reduce | flops 2949120 | bytes 17694720
  687.4 9.4 all_gather.49
  714.6 45.2 %reduce-scatter.37.cloned.1.call-done = f32[48,4]{1,0:T(8,128)} async-done(((f32[768,4]{1,0:T(8,128)}), f32[48,4]{1,0:T(8,128)}) %reduce-scatter.37.cloned.1.call-update) | async-done | bytes 784
  760.8 20.3 %all_gather.54 = bf16[2,2,768]{1,0,2:T(2,128)(2,1)S(1)} all-gather(bf16[2,2,48]{1,0,2:T(2,128)(2,1)S(1)} %copy.59), channel_id=1, replica_groups=mesh['dp'=16,'tensor'=2] {'dp'}, dimensions={2}, use_global_device_ids=true | all-gather | bytes 6528 | tf_op jit(solution)/shard_map/all_gather | solution.py:309
  782.0 36.2 %reduce-scatter.39.cloned.1.call-done = f32[48,4]{1,0:T(8,128)} async-done(((f32[768,4]{1,0:T(8,128)}), f32[48,4]{1,0:T(8,128)}) %reduce-scatter.39.cloned.1.call-update) | async-done | bytes 784
  819.2 20.3 %all_gather.55 = bf16[2,2,768]{1,0,2:T(2,128)(2,1)S(1)} all-gather(bf16[2,2,48]{1,0,2:T(2,128)(2,1)S(1)} %copy.60), channel_id=1, replica_groups=mesh['dp'=16,'tensor'=2] {'dp'}, dimensions={2}, use_global_device_ids=true | all-gather | bytes 6528 | tf_op jit(solution)/shard_map/all_gather | solution.py:312
  840.3 19.9 %all-gather.7.cloned.1.call-done = bf16[2,384,768]{1,0,2:T(2,128)(2,1)} async-done(((bf16[2,384,48]{1,0,2:T(2,128)(2,1)}), bf16[2,384,768]{1,0,2:T(2,128)(2,1)}) %all-gather.7.cloned.1.call-update) | async-done | bytes 1179664 | tf_op jit(solution)/shard_map/all_gather | solution.py:300
  865.3 50.2 %all-gather.11.cloned.1.call-done = bf16[2,1536,768]{1,0,2:T(2,128)(2,1)} async-done(((bf16[2,1536,48]{1,0,2:T(2,128)(2,1)}), bf16[2,1536,768]{1,0,2:T(2,128)(2,1)}) %all-gather.11.cloned.1.call-update) | async-done | bytes 4718608 | tf_op jit(solution)/shard_map/all_gather | solution.py:306
  915.5 13.7 %copy.62 = f32[2,1536,768]{2,1,0:T(8,128)} copy(bf16[2,1536,768]{1,0,2:T(2,128)(2,1)} %all-gather.11.cloned.1.call-done) | data formatting | bytes 14155776
  929.1 35.6 %all-gather.5.cloned.1.call-done = bf16[2,768,3,384]{3,1,2,0:T(8,128)(2,1)} async-done(((bf16[2,48,3,384]{3,1,2,0:T(8,128)(2,1)}), bf16[2,768,3,384]{3,1,2,0:T(8,128)(2,1)}) %all-gather.5.cloned.1.call-update) | async-done | bytes 3538960 | tf_op jit(solution)/shard_map/all_gather | solution.py:297
  964.7 5.5 convert_element_type.312
  970.2 48.4 %all-gather.9.cloned.1.call-done = bf16[2,768,1536]{2,1,0:T(8,128)(2,1)} async-done(((bf16[2,48,1536]{2,1,0:T(8,128)(2,1)}), bf16[2,768,1536]{2,1,0:T(8,128)(2,1)}) %all-gather.9.cloned.1.call-update) | async-done | bytes 4718608 | tf_op jit(solution)/shard_map/all_gather | solution.py:303
  1018.6 7.4 convert_element_type.316
  (306 shorter events, 177.8 us)
Async XLA Ops:
  7.2 39.9 %reduce-scatter.17.cloned.1.call-start = ((), (), s32[]{:S(2)}) async-start(), calls=%async_computation.12 | async-start | bytes 1179648 | tf_op jit(solution)/shard_map/reduce_scatter | solution.py:141
  11.0 85.7 %copy-start.49 = (f32[768]{0:T(1024)}, f32[768]{0:T(1024)S(1)}, u32[]{:S(2)}) copy-start(f32[768]{0:T(1024)S(1)} %get-tuple-element.130) | copy-start | bytes 9220
  11.1 126.6 %copy-start.45 = (f32[768]{0:T(1024)}, f32[768]{0:T(1024)S(1)}, u32[]{:S(2)}) copy-start(f32[768]{0:T(1024)S(1)} %get-tuple-element.127) | copy-start | bytes 9220
  14.2 7.1 copy-start.32
  26.8 31.1 %copy-start = (bf16[512,768]{1,0:T(8,128)(2,1)S(1)}, bf16[512,768]{1,0:T(8,128)(2,1)}, u32[]{:S(2)}) copy-start(bf16[512,768]{1,0:T(8,128)(2,1)} %param.8) | copy-start | bytes 2359300
  28.3 56.7 %reduce-scatter.19.cloned.1.call-start = ((), (), s32[]{:S(2)}) async-start(), calls=%async_computation.13 | async-start | bytes 1179648 | tf_op jit(solution)/shard_map/reduce_scatter | solution.py:154
  66.6 59.7 %reduce-scatter.21.cloned.1.call-start = ((), (), s32[]{:S(2)}) async-start(), calls=%async_computation.14 | async-start | bytes 1179648 | tf_op jit(solution)/shard_map/reduce_scatter | solution.py:141
  107.8 59.4 %reduce-scatter.25.cloned.1.call-start = ((), (), s32[]{:S(2)}) async-start(), calls=%async_computation.16 | async-start | bytes 1179648 | tf_op jit(solution)/shard_map/reduce_scatter | solution.py:200
  138.5 7.9 slice-start.8
  148.7 39.9 %reduce-scatter.23.cloned.1.call-start = ((), (), s32[]{:S(2)}) async-start(), calls=%async_computation.15 | async-start | bytes 1179648 | tf_op jit(solution)/shard_map/reduce_scatter | solution.py:154
  154.4 89.9 %reduce-scatter.27.cloned.1.call-start = ((), (), s32[]{:S(2)}) async-start(), calls=%async_computation.17 | async-start | bytes 1179648 | tf_op jit(solution)/shard_map/reduce_scatter | solution.py:230
  188.6 14.6 %copy-start.21 = (bf16[512,768]{1,0:T(8,128)(2,1)S(1)}, bf16[512,768]{1,0:T(8,128)(2,1)}, u32[]{:S(2)}) copy-start(bf16[512,768]{1,0:T(8,128)(2,1)} %param.15) | copy-start | bytes 2359300
  188.6 17.3 %slice-start = ((s8[6291456]{0:T(1024)(128)(4,1)}), s8[4194304]{0:T(1024)(128)(4,1)S(1)}, s32[]{:S(2)}) async-start(s8[6291456]{0:T(1024)(128)(4,1)} %bitcast.171), calls=%async_computation.28 | async-start | bytes 8388608
  199.9 6.0 slice-start.1
  226.2 60.0 %reduce-scatter.29.cloned.1.call-start = ((), (), s32[]{:S(2)}) async-start(), calls=%async_computation.18 | async-start | bytes 1179648 | tf_op jit(solution)/shard_map/reduce_scatter | solution.py:200
  257.2 8.1 slice-start.10
  259.4 5.9 slice-start.11
  267.6 419.7 %reduce-scatter.31.cloned.1.call-start = ((), (), s32[]{:S(2)}) async-start(), calls=%async_computation.19 | async-start | bytes 1179648 | tf_op jit(solution)/shard_map/reduce_scatter | solution.py:230
  286.1 12.7 %copy-start.11 = (f32[512,768]{1,0:T(8,128)S(1)}, f32[512,768]{1,0:T(8,128)}, u32[]{:S(2)}) copy-start(f32[512,768]{1,0:T(8,128)} %copy-done.10) | copy-start | bytes 4718596
  301.5 5.6 copy-start.33
  312.9 6.7 copy-start.27
  332.5 376.6 %reduce-scatter.33.cloned.1.call-start = ((), (), s32[]{:S(2)}) async-start(), calls=%async_computation.20 | async-start | bytes 7520256 | tf_op jit(solution)/shard_map/reduce_scatter | solution.py:289
  340.5 370.5 %reduce-scatter.35.cloned.1.call-start = ((), (), s32[]{:S(2)}) async-start(), calls=%async_computation.23 | async-start | bytes 10027008 | tf_op jit(solution)/shard_map/reduce_scatter | solution.py:291
  351.2 408.6 %reduce-scatter.37.cloned.1.call-start = ((), (), s32[]{:S(2)}) async-start(), calls=%async_computation.26 | async-start | bytes 417792
  364.8 15.6 %copy-start.6 = (f32[512,768]{1,0:T(8,128)S(1)}, f32[512,768]{1,0:T(8,128)}, u32[]{:S(2)}) copy-start(f32[512,768]{1,0:T(8,128)} %copy-done.5) | copy-start | bytes 4718596
  364.8 15.6 %copy-start.29 = (bf16[6,64,512]{2,1,0:T(8,128)(2,1)S(1)}, bf16[6,64,512]{2,1,0:T(8,128)(2,1)}, u32[]{:S(2)}) copy-start(bf16[6,64,512]{2,1,0:T(8,128)(2,1)} %copy-done.28) | copy-start | bytes 1179652
  687.4 10.0 copy-start.44
  701.9 116.3 %reduce-scatter.39.cloned.1.call-start = ((), (), s32[]{:S(2)}) async-start(), calls=%async_computation.27 | async-start | bytes 417792
  705.5 154.8 %all-gather.7.cloned.1.call-start = ((), (), s32[]{:S(2)}) async-start(), calls=%async_computation.22 | async-start | bytes 1253376 | tf_op jit(solution)/shard_map/all_gather | solution.py:300
  707.1 208.4 %all-gather.11.cloned.1.call-start = ((), (), s32[]{:S(2)}) async-start(), calls=%async_computation.25 | async-start | bytes 5013504 | tf_op jit(solution)/shard_map/all_gather | solution.py:306
  709.1 255.6 %all-gather.5.cloned.1.call-start = ((), (), s32[]{:S(2)}) async-start(), calls=%async_computation.21 | async-start | bytes 3760128 | tf_op jit(solution)/shard_map/all_gather | solution.py:297
  710.9 307.7 %all-gather.9.cloned.1.call-start = ((), (), s32[]{:S(2)}) async-start(), calls=%async_computation.24 | async-start | bytes 5013504 | tf_op jit(solution)/shard_map/all_gather | solution.py:303
  (56 other events, 149.1 us)
Sparse Core Ops, SparseCore 0:
  28.4 18.5 reduce-scatter.16
  66.7 18.2 reduce-scatter.18
  107.9 18.3 reduce-scatter.20
  148.8 18.3 reduce-scatter.24
  169.9 18.7 reduce-scatter.22
  226.3 18.0 reduce-scatter.26
  267.8 18.3 reduce-scatter.28
  332.6 18.2 reduce-scatter.30
  355.5 129.8 reduce-scatter.32
  490.0 166.6 reduce-scatter.34
  702.0 57.7 reduce-scatter.36
  763.5 54.5 reduce-scatter.38
  821.0 39.2 all-gather.6
  862.4 53.0 all-gather.10
  918.2 46.4 all-gather.4
  966.9 51.6 all-gather.8
where the time goes:
time: 1040 us; the launch traced here: 1030 us
  blocking collectives  426 us (41%)
  waiting for transfers between devices  348 us (33%)
  matrix products  95.8 us (9%)
  local copies, waits for them, and re-layouts  82.4 us (8%)
  other arithmetic  63.4 us (6%)
  between operations  16.2 us (2%)
    unnamed x1, blocking collectives  299 us
    unnamed x18, waiting for transfers between devices  81.6 us
    all_gather x1, waiting for transfers between devices, on_device(): lax.all_gather(shares[3].astype(jnp.bfloat16), 'dp', axis=2, tiled=True)  50.2 us
    all_gather x1, waiting for transfers between devices, on_device(): lax.all_gather(shares[2].astype(jnp.bfloat16), 'dp', axis=1, tiled=True)  48.4 us
    unnamed x157, local copies, waits for them, and re-layouts  45.2 us
    reduce_scatter x2, waiting for transfers between devices, layer_forward(): lax.psum_scatter(jnp.dot(attended, w_out, preferred_element_type=jnp.floa...  37.1 us
    all_gather x1, waiting for transfers between devices, on_device(): lax.all_gather(shares[0].astype(jnp.bfloat16), 'dp', axis=1, tiled=True)  35.6 us
    reduce_scatter x2, waiting for transfers between devices, layer_backward(): lax.psum_scatter(jnp.einsum('lf,df->ld', d_pre, w_up, preferred_element_t...  31.1 us
  transfers between devices with their start and end apart: 16, of which 13 were waited for; matrix products, arithmetic and copies ran while one was open for 10% of the time, Pallas kernels for 0%

commit v1 on v0

v1 whole, which is shorter than its diff:
```python
import jax
import jax.numpy as jnp
from jax import lax
from jax.sharding import PartitionSpec as P

HEAD_DIM = 64
SOFTNESS = 0.25
EPSILON = 1e-05
F32 = jnp.float32
BF16 = jnp.bfloat16


def mm(a, b, dims):
    return lax.dot_general(a, b, (dims, ((), ())), preferred_element_type=F32)


def nn(a, b):
    return mm(a, b, ((1,), (0,)))


def nt(a, b):
    return mm(a, b, ((1,), (1,)))


def tn(a, b):
    return mm(a, b, ((0,), (0,)))


def normalise(rows_in):
    row_mean = jnp.mean(rows_in, axis=-1, keepdims=True)
    centered = rows_in - row_mean
    spread = jnp.mean(centered * centered, axis=-1, keepdims=True)
    inverse = lax.rsqrt(spread + EPSILON)
    return centered * inverse, inverse


def norm_back(d_normed, unit, inverse, gain):
    scaled = d_normed * gain
    mean_one = jnp.mean(scaled, axis=-1, keepdims=True)
    mean_two = jnp.mean(scaled * unit, axis=-1, keepdims=True)
    return inverse * (scaled - mean_one - unit * mean_two)


def gelu_both(u):
    rate = 0.7978845608028654
    squared = u * u
    bend = jnp.tanh(rate * u * (1.0 + 0.044715 * squared))
    half = 0.5 * (1.0 + bend)
    slope = half + 0.5 * u * (1.0 - bend * bend) * rate * (1.0 + 3 * 0.044715 * squared)
    return u * half, slope


def scores_of(q, k, start, signed):
    scores = nt(q, k) * HEAD_DIM**-0.5
    rows = start + lax.broadcasted_iota(jnp.int32, scores.shape, 0)
    cols = lax.broadcasted_iota(jnp.int32, scores.shape, 1)
    allowed = cols <= rows
    if signed:
        inv_mag = lax.rsqrt(scores * scores + SOFTNESS * SOFTNESS)
        magnitude = (scores * scores + SOFTNESS * SOFTNESS) * inv_mag
    else:
        inv_mag, magnitude = None, scores
    masked = jnp.where(allowed, magnitude, -1e30)
    peak = jnp.max(masked, axis=-1, keepdims=True)
    exponent = jnp.exp(masked - peak)
    softmax_part = exponent / jnp.sum(exponent, axis=-1, keepdims=True)
    return scores, inv_mag, softmax_part


def head_forward(q, k, v, start, signed):
    scores, inv_mag, weights = scores_of(q, k, start, signed)
    if signed:
        weights = weights * (scores * inv_mag)
    return nn(weights.astype(BF16), v).astype(BF16)


def head_backward(q, k, v, d_att, start, signed):
    scores, inv_mag, part = scores_of(q, k, start, signed)
    d_probs = nt(d_att, v)
    if signed:
        sign = scores * inv_mag
        weights = part * sign
        bend = sign * sign + (SOFTNESS * SOFTNESS) * (inv_mag * inv_mag * inv_mag)
        delta = jnp.sum(weights * d_probs, axis=-1, keepdims=True)
        d_scores = part * (d_probs * bend - sign * delta)
    else:
        weights = part
        delta = jnp.sum(weights * d_probs, axis=-1, keepdims=True)
        d_scores = weights * (d_probs - delta)
    low = d_scores.astype(BF16)
    scale = HEAD_DIM**-0.5
    return nn(low, k) * scale, tn(low, q) * scale, tn(weights.astype(BF16), d_att)


def swap_tensor(v):
    return lax.ppermute(v, "tensor", [(0, 1), (1, 0)])


def half_of(v, which, axis):
    size = v.shape[axis] // 2
    return lax.dynamic_slice_in_dim(v, which * size, size, axis)


def joined(own, other, which, axis=0):
    first = which == 0
    return jnp.concatenate(
        [jnp.where(first, own, other), jnp.where(first, other, own)], axis=axis
    )


def pairs(count, step):
    return [(i, i ^ step) for i in range(count)]


def reduce_block(keep, send, place):
    core, x, z = place
    n_dp = 16
    total = keep + lax.ppermute(send, "dp", pairs(n_dp, 1)).astype(F32)
    low = total.astype(BF16)
    total = half_of(total, x, 0) + lax.ppermute(half_of(low, 1 - x, 0), "dp", pairs(n_dp, 2)).astype(F32)
    far = half_of(total, 1 - z // 2, 0)
    near = half_of(total, z // 2, 0)
    line = lambda moves: [(a * 4 + r, b * 4 + r) for a, b in moves for r in range(4)]
    out_to_in = lax.ppermute(far.astype(BF16), "dp", line([(0, 1), (3, 2)])).astype(F32)
    across = lax.ppermute((far + out_to_in).astype(BF16), "dp", line([(1, 2), (2, 1)])).astype(F32)
    near = near + across
    own = half_of(near, z % 2, 0)
    sibling = half_of(near, 1 - z % 2, 0).astype(BF16)
    own = own + lax.ppermute(sibling, "dp", pairs(n_dp, 4)).astype(F32)
    own = own.astype(BF16)
    near = joined(own, lax.ppermute(own, "dp", pairs(n_dp, 4)), z % 2)
    across = lax.ppermute(near, "dp", line([(1, 2), (2, 1)]))
    out = lax.ppermute(across, "dp", line([(1, 0), (2, 3)]))
    far = jnp.where((z == 1) | (z == 2), across, out)
    low = joined(near, far, z // 2)
    low = joined(low, lax.ppermute(low, "dp", pairs(n_dp, 2)), x)
    return low, lax.ppermute(low, "dp", pairs(n_dp, 1))


def reduce_any(keep, send, place, n_dp):
    if n_dp == 16:
        return reduce_block(keep, send, place)
    whole = lax.psum(joined(keep.astype(BF16), send, place[0]), "dp")
    return half_of(whole, place[0], 0), half_of(whole, 1 - place[0], 0)


def sum_small(v, n_dp):
    if n_dp == 16:
        for step in (1, 2, 4, 8):
            v = v + lax.ppermute(v, "dp", pairs(n_dp, step))
        return v + swap_tensor(v)
    return lax.psum(v, ("dp", "tensor"))


def attention_part(stream, gain, shift, w_qkv, earlier, signed):
    unit, inverse = normalise(stream)
    normed = (unit * gain + shift).astype(BF16)
    qkv = [nn(normed, w_qkv[c]).astype(BF16) for c in range(3)]
    keys = jnp.concatenate([b[1] for b in earlier] + [qkv[1]])
    values = jnp.concatenate([b[2] for b in earlier] + [qkv[2]])
    start = keys.shape[0] - stream.shape[0]
    heads = []
    for h in range(keys.shape[1] // HEAD_DIM):
        cut = slice(h * HEAD_DIM, (h + 1) * HEAD_DIM)
        heads.append(head_forward(qkv[0][:, cut], keys[:, cut], values[:, cut], start, signed))
    return normed, qkv, jnp.concatenate(heads, axis=1)


def mlp_part(middle, gain, shift, w_up, w_down):
    unit, inverse = normalise(middle)
    normed = (unit * gain + shift).astype(BF16)
    value, slope = gelu_both(nn(normed, w_up))
    hidden = value.astype(BF16)
    return normed, hidden, slope.astype(BF16), nn(hidden, w_down).astype(BF16)


def attention_back(d_att, blocks, row, signed):
    start = row * d_att.shape[0]
    keys = jnp.concatenate([b[1] for b in blocks[: row + 1]])
    values = jnp.concatenate([b[2] for b in blocks[: row + 1]])
    outs = []
    for h in range(keys.shape[1] // HEAD_DIM):
        cut = slice(h * HEAD_DIM, (h + 1) * HEAD_DIM)
        outs.append(
            head_backward(
                blocks[row][0][:, cut], keys[:, cut], values[:, cut], d_att[:, cut], start, signed
            )
        )
    return [jnp.concatenate(part, axis=1) for part in zip(*outs)]


def on_device(parts, n_dp, tokens, w_qkv, w_out, w_up, w_down, norm_gain, norm_shift, d_out):
    layers = w_qkv.shape[0]
    length = tokens.shape[0]
    size = length // parts
    cuts = [slice(r * size, (r + 1) * size) for r in range(parts)]
    w_qkv = jnp.transpose(w_qkv, (0, 2, 1, 3))
    index = lax.axis_index("dp")
    place = (index % 2, index // 2 % 2, index // 4)
    core = place[0]
    streams = [tokens[c].astype(F32) for c in cuts]
    saved = []
    outputs = []
    for l in range(layers):
        signed = l == 0
        blocks, normed_one, attended, middles, own_parts = [], [], [], [], []
        for r in range(parts):
            normed, qkv, att = attention_part(
                streams[r], norm_gain[l, 0], norm_shift[l, 0], w_qkv[l], blocks, signed
            )
            blocks.append(qkv)
            normed_one.append(normed)
            attended.append(att)
        for r in range(parts):
            partial = nn(attended[r], w_out[l]).astype(BF16)
            middles.append(streams[r] + (partial.astype(F32) + swap_tensor(partial).astype(F32)))
        mlp = []
        nexts = []
        for r in range(parts):
            mlp.append(mlp_part(middles[r], norm_gain[l, 1], norm_shift[l, 1], w_up[l], w_down[l]))
            partial = mlp[r][3]
            nexts.append(middles[r] + (partial.astype(F32) + swap_tensor(partial).astype(F32)))
        saved.append((streams, blocks, normed_one, attended, middles, mlp))
        streams = nexts
        outputs.append(jnp.concatenate([s.astype(BF16) for s in streams]))
    d_next = [d_out[c].astype(F32) for c in cuts]
    small = [[None] * 4 for _ in range(layers)]
    big = [None] * layers

    def row_sums(partials, units):
        own = [p.astype(F32) for p in partials]
        return (
            sum(jnp.sum(o * u, axis=0) for o, u in zip(own, units)),
            sum(jnp.sum(o, axis=0) for o in own),
        )

    for l in reversed(range(layers)):
        signed = l == 0
        streams, blocks, normed_one, attended, middles, mlp = saved[l]
        rows = range(parts)
        d_low = [d.astype(BF16) for d in d_next]
        d_pre = [
            (nt(d_low[r], w_down[l]) * mlp[r][2].astype(F32)).astype(BF16) for r in rows
        ]
        two_own = [nt(d, w_up[l]).astype(BF16) for d in d_pre]
        two_other = [swap_tensor(p) for p in two_own]
        hidden = jnp.concatenate([m[1] for m in mlp])
        normed_two = jnp.concatenate([m[0] for m in mlp])
        low_all, pre_all = jnp.concatenate(d_low), jnp.concatenate(d_pre)

        def mlp_grads(which):
            return jnp.concatenate(
                [tn(half_of(hidden, which, 1), low_all), tn(normed_two, half_of(pre_all, which, 1))],
                axis=1,
            )

        mlp_sum = reduce_any(mlp_grads(core), mlp_grads(1 - core).astype(BF16), place, n_dp)
        d_mid, mid_low, units = [], [], []
        for r in rows:
            unit, inverse = normalise(middles[r])
            units.append(unit)
            total = two_own[r].astype(F32) + two_other[r].astype(F32)
            d_mid.append(d_next[r] + norm_back(total, unit, inverse, norm_gain[l, 1]))
            mid_low.append(d_mid[r].astype(BF16))
        small[l][2:] = row_sums(two_own, units)
        d_qkv = [None] * parts
        carried = None
        for r in reversed(rows):
            d_att = nt(mid_low[r], w_out[l]).astype(BF16)
            d_q, d_k, d_v = attention_back(d_att, blocks, r, signed)
            if carried is not None:
                d_k, d_v = d_k + carried[0], d_v + carried[1]
            carried = (d_k[: r * size], d_v[: r * size])
            d_qkv[r] = [d_q.astype(BF16), d_k[r * size :].astype(BF16), d_v[r * size :].astype(BF16)]
        one_own = [
            sum(nt(d_qkv[r][c], w_qkv[l, c]) for c in range(3)).astype(BF16) for r in rows
        ]
        one_other = [swap_tensor(p) for p in one_own]
        att_all, mid_all = jnp.concatenate(attended), jnp.concatenate(mid_low)
        normed_all = jnp.concatenate(normed_one)
        qkv_all = [jnp.concatenate([d[c] for d in d_qkv]) for c in range(3)]

        def att_grads(which):
            lhs = half_of(normed_all, which, 1)
            return jnp.concatenate(
                [tn(lhs, d) for d in qkv_all] + [tn(att_all, half_of(mid_all, which, 1))], axis=1
            )

        att_sum = reduce_any(att_grads(core), att_grads(1 - core).astype(BF16), place, n_dp)
        big[l] = (mlp_sum, att_sum)
        units = []
        for r in rows:
            unit, inverse = normalise(streams[r])
            units.append(unit)
            total = one_own[r].astype(F32) + one_other[r].astype(F32)
            d_mid[r] = d_mid[r] + norm_back(total, unit, inverse, norm_gain[l, 0])
        small[l][:2] = row_sums(one_own, units)
        d_next = d_mid
    small_sum = sum_small(jnp.stack([s for row in small for s in row]), n_dp)
    small_sum = small_sum.reshape(layers, 2, 2, small_sum.shape[-1])
    width = tokens.shape[1]
    part = w_qkv.shape[3]
    g_qkv, g_out, g_up, g_down = [], [], [], []
    for l in range(layers):
        (own, other), (own_a, other_a) = big[l]
        both = lambda a, b, axis=0: joined(a.astype(F32), b.astype(F32), core, axis)
        g_down.append(both(own[:, :width], other[:, :width]))
        g_up.append(both(own[:, width:], other[:, width:], 1))
        g_qkv.append(
            jnp.stack(
                [
                    both(own_a[:, c * part : (c + 1) * part], other_a[:, c * part : (c + 1) * part])
                    for c in range(3)
                ]
            )
        )
        g_out.append(both(own_a[:, 3 * part :], other_a[:, 3 * part :], 1))
    return (
        outputs[0],
        outputs[1],
        jnp.concatenate(d_next),
        jnp.transpose(jnp.stack(g_qkv), (0, 2, 1, 3)),
        jnp.stack(g_out),
        jnp.stack(g_up),
        jnp.stack(g_down),
        small_sum[:, :, 0],
        small_sum[:, :, 1],
    )


def solution(mesh):
    n_dp = mesh.shape["dp"]
    in_specs = (
        P("dp", None),
        P(None, None, None, "tensor"),
        P(None, "tensor", None),
        P(None, None, "tensor"),
        P(None, "tensor", None),
        P(),
        P(),
        P("dp", None),
    )
    out_specs = (
        P("dp", None),
        P("dp", None),
        P("dp", None),
        P(None, None, None, "tensor"),
        P(None, "tensor", None),
        P(None, None, "tensor"),
        P(None, "tensor", None),
        P(),
        P(),
    )

    def body(*args):
        return on_device(1, n_dp, *args)

    return jax.shard_map(body, mesh=mesh, in_specs=in_specs, out_specs=out_specs, check_vma=False)
```

time: 1040 us -> 571 us (0.55)
  blocking collectives: 426 us -> 0 us
  waiting for transfers between devices: 348 us -> 204 us
  starting transfers between devices: 1.34 us -> 105 us
  other arithmetic: 63.4 us -> 108 us
  local copies, waits for them, and re-layouts: 82.4 us -> 60.9 us
  matrix products: 95.8 us -> 77.8 us
  between operations: 16.2 us -> 4.33 us
    unnamed x1 -> x0, blocking collectives: 299 us -> none
    ppermute x0 -> x53, waiting for transfers between devices: none -> 204 us  [the longest x9 72.1 us: swap_tensor(): return lax.ppermute(v, 'tensor', [(0, 1), (1, 0)])]
    all_gather x4 -> x0, waiting for transfers between devices: 154 us -> none  [the longest x1 50.2 us: on_device(): lax.all_gather(shares[3].astype(jnp.bfloat16), 'dp', axis=2, tiled=True)]
    all_gather x10 -> x0, blocking collectives: 127 us -> none  [the longest x2 22.3 us: layer_forward(): lax.all_gather(mixed_share.astype(jnp.bfloat16), 'tensor', axis=0, tiled=...]
    reduce_scatter x10 -> x0, waiting for transfers between devices: 112 us -> none  [the longest x2 37.1 us: layer_forward(): lax.psum_scatter(jnp.dot(attended, w_out, preferred_element_type=jnp.floa...]
    ppermute x0 -> x53, starting transfers between devices: none -> 105 us  [the longest x4 21.6 us: reduce_block(): return (low, lax.ppermute(low, 'dp', pairs(n_dp, 1)))]
    unnamed x18 -> x0, waiting for transfers between devices: 81.6 us -> none
    another operation x6 -> x9, local copies, waits for them, and re-layouts: 28.6 us -> 3.59 us  [on_device(): small_sum = sum_small(jnp.stack([s for row in small for s in row]), n_dp)]
  transfers between devices with their start and end apart: 16 -> 53, of which waited for: 13 -> 25; matrix products, arithmetic and copies ran while one was open for 10% -> 30% of each run, Pallas kernels for 0% -> 0%
where the time goes in v1:
time: 571 us; the launch traced here: 560 us
  waiting for transfers between devices  204 us (36%)
  other arithmetic  108 us (19%)
  starting transfers between devices  105 us (18%)
  matrix products  77.8 us (14%)
  local copies, waits for them, and re-layouts  60.9 us (11%)
    dot_general x120, matrix products, mm(): return lax.dot_general(a, b, (dims, ((), ())), preferred_element_type=F32)  77.8 us
    ppermute x9, waiting for transfers between devices, swap_tensor(): return lax.ppermute(v, 'tensor', [(0, 1), (1, 0)])  72.1 us
    ppermute x4, waiting for transfers between devices, reduce_block(): low = joined(low, lax.ppermute(low, 'dp', pairs(n_dp, 2)), x)  47.4 us
    unnamed x398, local copies, waits for them, and re-layouts  40.2 us
    ppermute x4, waiting for transfers between devices, reduce_block(): near = joined(own, lax.ppermute(own, 'dp', pairs(n_dp, 4)), z % 2)  24.5 us
    ppermute x4, starting transfers between devices, reduce_block(): return (low, lax.ppermute(low, 'dp', pairs(n_dp, 1)))  21.6 us
    ppermute x4, starting transfers between devices, reduce_block(): total = keep + lax.ppermute(send, 'dp', pairs(n_dp, 1)).astype(F32)  17.4 us
    select_n x16, other arithmetic, joined(): jnp.where(first, own, other)  14.7 us
  transfers between devices with their start and end apart: 53, of which 25 were waited for; matrix products, arithmetic and copies ran while one was open for 30% of the time, Pallas kernels for 0%

profile of v1, /device:TPU:9, one launch (start us, length us, event | category | flops | bytes accessed | tf_op | source)
XLA Modules:
  0.0 560.3 jit_solution(5240442587433534893)
XLA Ops:
  18.1 17.2 %collective-permute-done = bf16[512,768]{1,0:T(8,128)(2,1)S(1)} collective-permute-done((bf16[512,768]{1,0:T(8,128)(2,1)S(1)}, bf16[512,768]{1,0:T(8,128)(2,1)S(1)}, u32[]{:S(2)}, u32[]{:S(2)}) %collective-permute-start) | collective-permute-done | bytes 786464 | tf_op jit(solution)/shard_map/ppermute | solution.py:96
  43.0 16.3 %collective-permute-done.1 = bf16[512,768]{1,0:T(8,128)(2,1)S(1)} collective-permute-done((bf16[512,768]{1,0:T(8,128)(2,1)S(1)}, bf16[512,768]{1,0:T(8,128)(2,1)S(1)}, u32[]{:S(2)}, u32[]{:S(2)}) %collective-permute-start.1) | collective-permute-done | bytes 786464 | tf_op jit(solution)/shard_map/ppermute | solution.py:96
  70.5 15.7 %collective-permute-done.2 = bf16[512,768]{1,0:T(8,128)(2,1)} collective-permute-done((bf16[512,768]{1,0:T(8,128)(2,1)}, bf16[512,768]{1,0:T(8,128)(2,1)}, u32[]{:S(2)}, u32[]{:S(2)}) %collective-permute-start.2) | collective-permute-done | bytes 786464 | tf_op jit(solution)/shard_map/ppermute | solution.py:96
  88.9 3.7 multiply_convert_fusion
  107.7 3.9 collective-permute-start.38
  113.5 16.0 %collective-permute-done.3 = bf16[512,768]{1,0:T(8,128)(2,1)S(1)} collective-permute-done((bf16[512,768]{1,0:T(8,128)(2,1)S(1)}, bf16[512,768]{1,0:T(8,128)(2,1)S(1)}, u32[]{:S(2)}, u32[]{:S(2)}) %collective-permute-start.3) | collective-permute-done | bytes 786464 | tf_op jit(solution)/shard_map/ppermute | solution.py:96
  153.2 4.7 collective-permute-start.18
  160.6 6.0 %collective-permute-done.5 = bf16[512,768]{1,0:T(8,128)(2,1)S(1)} collective-permute-done((bf16[512,768]{1,0:T(8,128)(2,1)S(1)}, bf16[512,768]{1,0:T(8,128)(2,1)S(1)}, u32[]{:S(2)}, u32[]{:S(2)}) %collective-permute-start.5) | collective-permute-done | bytes 786464 | tf_op jit(solution)/shard_map/ppermute | solution.py:96
  181.0 5.5 collective-permute-start.28
  256.0 4.6 collective-permute-start.48
  265.1 7.1 %collective-permute-done.50 = f32[8,768]{1,0:T(8,128)S(1)} collective-permute-done((f32[8,768]{1,0:T(8,128)S(1)}, f32[8,768]{1,0:T(8,128)S(1)}, u32[]{:S(2)}, u32[]{:S(2)}) %collective-permute-start.50) | collective-permute-done | bytes 24608 | tf_op jit(solution)/shard_map/ppermute | solution.py:150
  272.2 3.5 collective-permute-done.51
  281.4 5.2 collective-permute-done.23
  303.3 4.8 collective-permute-start.25
  332.5 20.9 %collective-permute-done.26 = bf16[192,1536]{1,0:T(8,128)(2,1)} collective-permute-done((bf16[192,1536]{1,0:T(8,128)(2,1)}, bf16[192,1536]{1,0:T(8,128)(2,1)}, u32[]{:S(2)}, u32[]{:S(2)}) %collective-permute-start.26) | collective-permute-done | bytes 589856 | tf_op jit(solution)/shard_map/ppermute | solution.py:136
  356.8 4.8 collective-permute-start.27
  364.8 8.2 %collective-permute-done.12 = bf16[48,1536]{0,1:T(8,128)(2,1)S(1)} collective-permute-done((bf16[48,1536]{0,1:T(8,128)(2,1)S(1)}, bf16[48,1536]{0,1:T(8,128)(2,1)S(1)}, u32[]{:S(2)}, u32[]{:S(2)}) %collective-permute-start.12) | collective-permute-done | bytes 147488 | tf_op jit(solution)/shard_map/ppermute | solution.py:129
  374.9 8.3 %collective-permute-done.13 = bf16[48,1536]{0,1:T(8,128)(2,1)S(1)} collective-permute-done((bf16[48,1536]{0,1:T(8,128)(2,1)S(1)}, bf16[48,1536]{0,1:T(8,128)(2,1)S(1)}, u32[]{:S(2)}, u32[]{:S(2)}) %collective-permute-start.13) | collective-permute-done | bytes 147488 | tf_op jit(solution)/shard_map/ppermute | solution.py:131
  394.0 4.0 collective-permute-start.15
  404.5 5.5 collective-permute-done.30
  420.8 7.0 %collective-permute-done.31 = bf16[192,1536]{1,0:T(8,128)(2,1)} collective-permute-done((bf16[192,1536]{1,0:T(8,128)(2,1)}, bf16[192,1536]{1,0:T(8,128)(2,1)}, u32[]{:S(2)}, u32[]{:S(2)}) %collective-permute-start.31) | collective-permute-done | bytes 589856 | tf_op jit(solution)/shard_map/ppermute | solution.py:125
  432.4 4.4 collective-permute-start.45
  441.8 10.9 %collective-permute-done.33 = bf16[96,1536]{1,0:T(8,128)(2,1)S(1)} collective-permute-done((bf16[96,1536]{1,0:T(8,128)(2,1)S(1)}, bf16[96,1536]{1,0:T(8,128)(2,1)S(1)}, u32[]{:S(2)}, u32[]{:S(2)}) %collective-permute-start.33) | collective-permute-done | bytes 294944 | tf_op jit(solution)/shard_map/ppermute | solution.py:131
  456.9 9.8 %collective-permute-done.34 = bf16[192,1536]{1,0:T(8,128)(2,1)S(1)} collective-permute-done((bf16[192,1536]{1,0:T(8,128)(2,1)S(1)}, bf16[192,1536]{1,0:T(8,128)(2,1)S(1)}, u32[]{:S(2)}, u32[]{:S(2)}) %collective-permute-start.34) | collective-permute-done | bytes 589856 | tf_op jit(solution)/shard_map/ppermute | solution.py:132
  470.5 6.4 %collective-permute-done.35 = bf16[192,1536]{1,0:T(8,128)(2,1)S(1)} collective-permute-done((bf16[192,1536]{1,0:T(8,128)(2,1)S(1)}, bf16[192,1536]{1,0:T(8,128)(2,1)S(1)}, u32[]{:S(2)}, u32[]{:S(2)}) %collective-permute-start.35) | collective-permute-done | bytes 589856 | tf_op jit(solution)/shard_map/ppermute | solution.py:133
  477.3 14.3 %collective-permute-done.46 = bf16[384,1536]{1,0:T(8,128)(2,1)S(1)} collective-permute-done((bf16[384,1536]{1,0:T(8,128)(2,1)S(1)}, bf16[384,1536]{1,0:T(8,128)(2,1)S(1)}, u32[]{:S(2)}, u32[]{:S(2)}) %collective-permute-start.46) | collective-permute-done | bytes 1179680 | tf_op jit(solution)/shard_map/ppermute | solution.py:136
  494.3 9.4 %collective-permute-start.47 = (bf16[768,1536]{1,0:T(8,128)(2,1)}, bf16[768,1536]{1,0:T(8,128)(2,1)}, u32[]{:S(2)}, u32[]{:S(2)}) collective-permute-start(bf16[768,1536]{1,0:T(8,128)(2,1)} %pad_maximum_fusion.3), channel_id=1, source_target_pairs={{0,2},{2,0},{4,6},{6,4},{8,10},{10,8},{12,14},{14,12},{16,18},{18,... | collective-permute-start | bytes 7077896 | tf_op jit(solution)/shard_map/ppermute | solution.py:137
  504.8 12.1 %collective-permute-done.36 = bf16[384,1536]{1,0:T(8,128)(2,1)S(1)} collective-permute-done((bf16[384,1536]{1,0:T(8,128)(2,1)S(1)}, bf16[384,1536]{1,0:T(8,128)(2,1)S(1)}, u32[]{:S(2)}, u32[]{:S(2)}) %collective-permute-start.36) | collective-permute-done | bytes 1179680 | tf_op jit(solution)/shard_map/ppermute | solution.py:136
  519.5 4.9 collective-permute-start.37
  535.5 8.2 %copy.71 = f32[2,768,3,384]{3,1,2,0:T(8,128)} copy(f32[2,768,3,384]{1,3,2,0:T(8,128)} %maximum_bitcast_fusion) | data formatting | bytes 14155776
  550.2 4.3 pad_maximum_fusion.1
  555.3 4.6 pad_maximum_fusion
  (772 shorter events, 293.6 us)
Async XLA Ops:
  16.8 18.5 %collective-permute-start = (bf16[512,768]{1,0:T(8,128)(2,1)S(1)}, bf16[512,768]{1,0:T(8,128)(2,1)S(1)}, u32[]{:S(2)}, u32[]{:S(2)}) collective-permute-start(bf16[512,768]{1,0:T(8,128)(2,1)S(1)} %convolution_convert_fusion.5), channel_id=1, source_target_pairs={{0,1},{1,0},{2,3},{3,2},{4,5},{5,4},{6,7},{7,6},{8,9},{9,8},{10,11... | collective-permute-start | bytes 2359304 | tf_op jit(solution)/shard_map/ppermute | solution.py:96
  41.8 17.6 %collective-permute-start.1 = (bf16[512,768]{1,0:T(8,128)(2,1)S(1)}, bf16[512,768]{1,0:T(8,128)(2,1)S(1)}, u32[]{:S(2)}, u32[]{:S(2)}) collective-permute-start(bf16[512,768]{1,0:T(8,128)(2,1)S(1)} %fusion.47), channel_id=1, source_target_pairs={{0,1},{1,0},{2,3},{3,2},{4,5},{5,4},{6,7},{7,6},{8,9},{9,8},{10,11... | collective-permute-start | bytes 2359304 | tf_op jit(solution)/shard_map/ppermute | solution.py:96
  69.3 16.9 %collective-permute-start.2 = (bf16[512,768]{1,0:T(8,128)(2,1)}, bf16[512,768]{1,0:T(8,128)(2,1)}, u32[]{:S(2)}, u32[]{:S(2)}) collective-permute-start(bf16[512,768]{1,0:T(8,128)(2,1)} %convolution_convert_fusion.4), channel_id=1, source_target_pairs={{0,1},{1,0},{2,3},{3,2},{4,5},{5,4},{6,7},{7,6},{8,9},{9,8},{10,11... | collective-permute-start | bytes 2359304 | tf_op jit(solution)/shard_map/ppermute | solution.py:96
  97.0 15.7 %collective-permute-start.4 = (bf16[512,768]{1,0:T(8,128)(2,1)S(1)}, bf16[512,768]{1,0:T(8,128)(2,1)S(1)}, u32[]{:S(2)}, u32[]{:S(2)}) collective-permute-start(bf16[512,768]{1,0:T(8,128)(2,1)S(1)} %fusion.50), channel_id=1, source_target_pairs={{0,1},{1,0},{2,3},{3,2},{4,5},{5,4},{6,7},{7,6},{8,9},{9,8},{10,11... | collective-permute-start | bytes 2359304 | tf_op jit(solution)/shard_map/ppermute | solution.py:96
  99.6 29.9 %collective-permute-start.3 = (bf16[512,768]{1,0:T(8,128)(2,1)S(1)}, bf16[512,768]{1,0:T(8,128)(2,1)S(1)}, u32[]{:S(2)}, u32[]{:S(2)}) collective-permute-start(bf16[512,768]{1,0:T(8,128)(2,1)S(1)} %fusion.53), channel_id=1, source_target_pairs={{0,1},{1,0},{2,3},{3,2},{4,5},{5,4},{6,7},{7,6},{8,9},{9,8},{10,11... | collective-permute-start | bytes 2359304 | tf_op jit(solution)/shard_map/ppermute | solution.py:96
  107.7 118.0 %collective-permute-start.38 = (bf16[768,1536]{1,0:T(8,128)(2,1)}, bf16[768,1536]{1,0:T(8,128)(2,1)}, u32[]{:S(2)}, u32[]{:S(2)}) collective-permute-start(bf16[768,1536]{1,0:T(8,128)(2,1)} %pad_maximum_fusion.6), channel_id=1, source_target_pairs={{0,2},{2,0},{4,6},{6,4},{8,10},{10,8},{12,14},{14,12},{16,18},{18,... | collective-permute-start | bytes 7077896 | tf_op jit(solution)/shard_map/ppermute | solution.py:118
  153.2 37.9 %collective-permute-start.18 = (bf16[384,1536]{0,1:T(8,128)(2,1)S(1)}, bf16[384,1536]{0,1:T(8,128)(2,1)S(1)}, u32[]{:S(2)}, u32[]{:S(2)}) collective-permute-start(bf16[384,1536]{0,1:T(8,128)(2,1)S(1)} %pad_maximum_fusion.10), channel_id=1, source_target_pairs={{0,2},{2,0},{4,6},{6,4},{8,10},{10,8},{12,14},{14,12},{16,18},{18,... | collective-permute-start | bytes 3538952 | tf_op jit(solution)/shard_map/ppermute | solution.py:118
  176.1 19.1 %collective-permute-start.6 = (bf16[512,768]{1,0:T(8,128)(2,1)S(1)}, bf16[512,768]{1,0:T(8,128)(2,1)}, u32[]{:S(2)}, u32[]{:S(2)}) collective-permute-start(bf16[512,768]{1,0:T(8,128)(2,1)S(1)} %fusion.44), channel_id=1, source_target_pairs={{0,1},{1,0},{2,3},{3,2},{4,5},{5,4},{6,7},{7,6},{8,9},{9,8},{10,11... | collective-permute-start | bytes 2359304 | tf_op jit(solution)/shard_map/ppermute | solution.py:96
  181.0 127.1 %collective-permute-start.28 = (bf16[768,1536]{1,0:T(8,128)(2,1)}, bf16[768,1536]{1,0:T(8,128)(2,1)}, u32[]{:S(2)}, u32[]{:S(2)}) collective-permute-start(bf16[768,1536]{1,0:T(8,128)(2,1)} %pad_maximum_fusion.5), channel_id=1, source_target_pairs={{0,2},{2,0},{4,6},{6,4},{8,10},{10,8},{12,14},{14,12},{16,18},{18,... | collective-permute-start | bytes 7077896 | tf_op jit(solution)/shard_map/ppermute | solution.py:118
  194.0 42.1 %collective-permute-start.19 = (bf16[192,1536]{1,0:T(8,128)(2,1)}, bf16[192,1536]{1,0:T(8,128)(2,1)}, u32[]{:S(2)}, u32[]{:S(2)}) collective-permute-start(bf16[192,1536]{1,0:T(8,128)(2,1)} %copy.58), channel_id=1, source_target_pairs={{0,4},{2,6},{4,0},{6,2},{8,12},{10,14},{12,8},{14,10},{16,20},{18,... | collective-permute-start | bytes 1769480 | tf_op jit(solution)/shard_map/ppermute | solution.py:120
  221.0 31.4 %collective-permute-start.7 = (bf16[512,768]{1,0:T(8,128)(2,1)}, bf16[512,768]{1,0:T(8,128)(2,1)}, u32[]{:S(2)}, u32[]{:S(2)}) collective-permute-start(bf16[512,768]{1,0:T(8,128)(2,1)} %add_convert_fusion.2), channel_id=1, source_target_pairs={{0,1},{1,0},{2,3},{3,2},{4,5},{5,4},{6,7},{7,6},{8,9},{9,8},{10,11... | collective-permute-start | bytes 2359304 | tf_op jit(solution)/shard_map/ppermute | solution.py:96
  233.2 57.0 %collective-permute-start.39 = (bf16[384,1536]{1,0:T(8,128)(2,1)}, bf16[384,1536]{1,0:T(8,128)(2,1)}, u32[]{:S(2)}, u32[]{:S(2)}) collective-permute-start(bf16[384,1536]{1,0:T(8,128)(2,1)} %dynamic-slice_convert_fusion), channel_id=1, source_target_pairs={{0,4},{2,6},{4,0},{6,2},{8,12},{10,14},{12,8},{14,10},{16,20},{18,... | collective-permute-start | bytes 3538952 | tf_op jit(solution)/shard_map/ppermute | solution.py:120
  242.4 54.1 %collective-permute-start.8 = (bf16[384,1536]{0,1:T(8,128)(2,1)}, bf16[384,1536]{0,1:T(8,128)(2,1)}, u32[]{:S(2)}, u32[]{:S(2)}) collective-permute-start(bf16[384,1536]{0,1:T(8,128)(2,1)} %pad_maximum_fusion.9), channel_id=1, source_target_pairs={{0,2},{2,0},{4,6},{6,4},{8,10},{10,8},{12,14},{14,12},{16,18},{18,... | collective-permute-start | bytes 3538952 | tf_op jit(solution)/shard_map/ppermute | solution.py:118
  263.5 16.1 %collective-permute-start.22 = (bf16[48,1536]{0,1:T(8,128)(2,1)S(1)}, bf16[48,1536]{0,1:T(8,128)(2,1)S(1)}, u32[]{:S(2)}, u32[]{:S(2)}) collective-permute-start(bf16[48,1536]{0,1:T(8,128)(2,1)S(1)} %dynamic-slice_convert_fusion.6), channel_id=1, source_target_pairs={{0,8},{2,10},{4,12},{6,14},{8,0},{10,2},{12,4},{14,6},{16,24},{18,... | collective-permute-start | bytes 442376 | tf_op jit(solution)/shard_map/ppermute | solution.py:129
  286.9 16.4 %collective-permute-start.24 = (bf16[96,1536]{0,1:T(8,128)(2,1)S(1)}, bf16[96,1536]{0,1:T(8,128)(2,1)}, u32[]{:S(2)}, u32[]{:S(2)}) collective-permute-start(bf16[96,1536]{0,1:T(8,128)(2,1)S(1)} %pad_maximum_fusion.18), channel_id=1, source_target_pairs={{8,16},{10,18},{12,20},{14,22},{16,8},{18,10},{20,12},{22,14},{9,1... | collective-permute-start | bytes 884744 | tf_op jit(solution)/shard_map/ppermute | solution.py:132
  294.9 26.2 %collective-permute-start.40 = (bf16[192,1536]{1,0:T(8,128)(2,1)}, bf16[192,1536]{1,0:T(8,128)(2,1)}, u32[]{:S(2)}, u32[]{:S(2)}) collective-permute-start(bf16[192,1536]{1,0:T(8,128)(2,1)} %dynamic-slice_convert_fusion.4), channel_id=1, source_target_pairs={{0,8},{2,10},{4,12},{6,14},{24,16},{26,18},{28,20},{30,22},{1,9},{... | collective-permute-start | bytes 1769480 | tf_op jit(solution)/shard_map/ppermute | solution.py:124
  302.7 14.9 %collective-permute-start.9 = (bf16[192,1536]{1,0:T(8,128)(2,1)}, bf16[192,1536]{1,0:T(8,128)(2,1)}, u32[]{:S(2)}, u32[]{:S(2)}) collective-permute-start(bf16[192,1536]{1,0:T(8,128)(2,1)} %copy.53), channel_id=1, source_target_pairs={{0,4},{2,6},{4,0},{6,2},{8,12},{10,14},{12,8},{14,10},{16,20},{18,... | collective-permute-start | bytes 1769480 | tf_op jit(solution)/shard_map/ppermute | solution.py:120
  312.5 78.5 %collective-permute-start.29 = (bf16[384,1536]{1,0:T(8,128)(2,1)}, bf16[384,1536]{1,0:T(8,128)(2,1)}, u32[]{:S(2)}, u32[]{:S(2)}) collective-permute-start(bf16[384,1536]{1,0:T(8,128)(2,1)} %dynamic-slice_convert_fusion.1), channel_id=1, source_target_pairs={{0,4},{2,6},{4,0},{6,2},{8,12},{10,14},{12,8},{14,10},{16,20},{18,... | collective-permute-start | bytes 3538952 | tf_op jit(solution)/shard_map/ppermute | solution.py:120
  317.0 36.5 %collective-permute-start.26 = (bf16[192,1536]{1,0:T(8,128)(2,1)}, bf16[192,1536]{1,0:T(8,128)(2,1)}, u32[]{:S(2)}, u32[]{:S(2)}) collective-permute-start(bf16[192,1536]{1,0:T(8,128)(2,1)} %copy.60), channel_id=1, source_target_pairs={{0,4},{2,6},{4,0},{6,2},{8,12},{10,14},{12,8},{14,10},{16,20},{18,... | collective-permute-start | bytes 1769480 | tf_op jit(solution)/shard_map/ppermute | solution.py:136
  323.2 40.4 %collective-permute-start.41 = (bf16[192,1536]{1,0:T(8,128)(2,1)}, bf16[192,1536]{1,0:T(8,128)(2,1)}, u32[]{:S(2)}, u32[]{:S(2)}) collective-permute-start(bf16[192,1536]{1,0:T(8,128)(2,1)} %add_convert_fusion.8), channel_id=1, source_target_pairs={{8,16},{10,18},{12,20},{14,22},{16,8},{18,10},{20,12},{22,14},{9,1... | collective-permute-start | bytes 1769480 | tf_op jit(solution)/shard_map/ppermute | solution.py:125
  329.8 31.9 %collective-permute-start.11 = (bf16[96,1536]{0,1:T(8,128)(2,1)}, bf16[96,1536]{0,1:T(8,128)(2,1)S(1)}, u32[]{:S(2)}, u32[]{:S(2)}) collective-permute-start(bf16[96,1536]{0,1:T(8,128)(2,1)} %add_convert_fusion.13), channel_id=1, source_target_pairs={{8,16},{10,18},{12,20},{14,22},{16,8},{18,10},{20,12},{22,14},{9,1... | collective-permute-start | bytes 884744 | tf_op jit(solution)/shard_map/ppermute | solution.py:125
  356.8 59.0 %collective-permute-start.27 = (bf16[384,1536]{0,1:T(8,128)(2,1)}, bf16[384,1536]{0,1:T(8,128)(2,1)}, u32[]{:S(2)}, u32[]{:S(2)}) collective-permute-start(bf16[384,1536]{0,1:T(8,128)(2,1)} %pad_maximum_fusion.8), channel_id=1, source_target_pairs={{0,2},{2,0},{4,6},{6,4},{8,10},{10,8},{12,14},{14,12},{16,18},{18,... | collective-permute-start | bytes 3538952 | tf_op jit(solution)/shard_map/ppermute | solution.py:137
  392.7 17.4 %collective-permute-start.30 = (bf16[192,1536]{1,0:T(8,128)(2,1)S(1)}, bf16[192,1536]{1,0:T(8,128)(2,1)S(1)}, u32[]{:S(2)}, u32[]{:S(2)}) collective-permute-start(bf16[192,1536]{1,0:T(8,128)(2,1)S(1)} %dynamic-slice_convert_fusion.5), channel_id=1, source_target_pairs={{0,8},{2,10},{4,12},{6,14},{24,16},{26,18},{28,20},{30,22},{1,9},{... | collective-permute-start | bytes 1769480 | tf_op jit(solution)/shard_map/ppermute | solution.py:124
  399.1 33.3 %collective-permute-start.44 = (bf16[192,1536]{1,0:T(8,128)(2,1)}, bf16[192,1536]{1,0:T(8,128)(2,1)}, u32[]{:S(2)}, u32[]{:S(2)}) collective-permute-start(bf16[192,1536]{1,0:T(8,128)(2,1)} %pad_maximum_fusion.16), channel_id=1, source_target_pairs={{8,16},{10,18},{12,20},{14,22},{16,8},{18,10},{20,12},{22,14},{9,1... | collective-permute-start | bytes 1769480 | tf_op jit(solution)/shard_map/ppermute | solution.py:132
  411.0 16.8 %collective-permute-start.31 = (bf16[192,1536]{1,0:T(8,128)(2,1)}, bf16[192,1536]{1,0:T(8,128)(2,1)}, u32[]{:S(2)}, u32[]{:S(2)}) collective-permute-start(bf16[192,1536]{1,0:T(8,128)(2,1)} %add_convert_fusion.9), channel_id=1, source_target_pairs={{8,16},{10,18},{12,20},{14,22},{16,8},{18,10},{20,12},{22,14},{9,1... | collective-permute-start | bytes 1769480 | tf_op jit(solution)/shard_map/ppermute | solution.py:125
  415.2 21.6 %collective-permute-start.16 = (bf16[192,1536]{1,0:T(8,128)(2,1)}, bf16[192,1536]{1,0:T(8,128)(2,1)}, u32[]{:S(2)}, u32[]{:S(2)}) collective-permute-start(bf16[192,1536]{1,0:T(8,128)(2,1)} %copy.55), channel_id=1, source_target_pairs={{0,4},{2,6},{4,0},{6,2},{8,12},{10,14},{12,8},{14,10},{16,20},{18,... | collective-permute-start | bytes 1769480 | tf_op jit(solution)/shard_map/ppermute | solution.py:136
  432.4 23.1 %collective-permute-start.45 = (bf16[192,1536]{1,0:T(8,128)(2,1)}, bf16[192,1536]{1,0:T(8,128)(2,1)}, u32[]{:S(2)}, u32[]{:S(2)}) collective-permute-start(bf16[192,1536]{1,0:T(8,128)(2,1)} %collective-permute-done.44), channel_id=1, source_target_pairs={{8,0},{10,2},{12,4},{14,6},{16,24},{18,26},{20,28},{22,30},{9,1},{... | collective-permute-start | bytes 1769480 | tf_op jit(solution)/shard_map/ppermute | solution.py:133
  439.3 29.0 %collective-permute-start.17 = (bf16[384,1536]{0,1:T(8,128)(2,1)S(1)}, bf16[384,1536]{0,1:T(8,128)(2,1)S(1)}, u32[]{:S(2)}, u32[]{:S(2)}) collective-permute-start(bf16[384,1536]{0,1:T(8,128)(2,1)S(1)} %pad_maximum_fusion.7), channel_id=1, source_target_pairs={{0,2},{2,0},{4,6},{6,4},{8,10},{10,8},{12,14},{14,12},{16,18},{18,... | collective-permute-start | bytes 3538952 | tf_op jit(solution)/shard_map/ppermute | solution.py:137
  468.1 23.5 %collective-permute-start.46 = (bf16[384,1536]{1,0:T(8,128)(2,1)S(1)}, bf16[384,1536]{1,0:T(8,128)(2,1)S(1)}, u32[]{:S(2)}, u32[]{:S(2)}) collective-permute-start(bf16[384,1536]{1,0:T(8,128)(2,1)S(1)} %pad_maximum_fusion.12), channel_id=1, source_target_pairs={{0,4},{2,6},{4,0},{6,2},{8,12},{10,14},{12,8},{14,10},{16,20},{18,... | collective-permute-start | bytes 3538952 | tf_op jit(solution)/shard_map/ppermute | solution.py:136
  477.2 39.7 %collective-permute-start.36 = (bf16[384,1536]{1,0:T(8,128)(2,1)S(1)}, bf16[384,1536]{1,0:T(8,128)(2,1)S(1)}, u32[]{:S(2)}, u32[]{:S(2)}) collective-permute-start(bf16[384,1536]{1,0:T(8,128)(2,1)S(1)} %pad_maximum_fusion.11), channel_id=1, source_target_pairs={{0,4},{2,6},{4,0},{6,2},{8,12},{10,14},{12,8},{14,10},{16,20},{18,... | collective-permute-start | bytes 3538952 | tf_op jit(solution)/shard_map/ppermute | solution.py:136
  494.3 49.4 %collective-permute-start.47 = (bf16[768,1536]{1,0:T(8,128)(2,1)}, bf16[768,1536]{1,0:T(8,128)(2,1)}, u32[]{:S(2)}, u32[]{:S(2)}) collective-permute-start(bf16[768,1536]{1,0:T(8,128)(2,1)} %pad_maximum_fusion.3), channel_id=1, source_target_pairs={{0,2},{2,0},{4,6},{6,4},{8,10},{10,8},{12,14},{14,12},{16,18},{18,... | collective-permute-start | bytes 7077896 | tf_op jit(solution)/shard_map/ppermute | solution.py:137
  519.5 27.4 %collective-permute-start.37 = (bf16[768,1536]{1,0:T(8,128)(2,1)}, bf16[768,1536]{1,0:T(8,128)(2,1)}, u32[]{:S(2)}, u32[]{:S(2)}) collective-permute-start(bf16[768,1536]{1,0:T(8,128)(2,1)} %pad_maximum_fusion.2), channel_id=1, source_target_pairs={{0,2},{2,0},{4,6},{6,4},{8,10},{10,8},{12,14},{14,12},{16,18},{18,... | collective-permute-start | bytes 7077896 | tf_op jit(solution)/shard_map/ppermute | solution.py:137
  (218 other events, 1022.6 us)
